TPU v7x, 512 devices: a whole 4x4x16 slice. The times are simulated.
512 devices in a mesh: train: 16 (over z_lo, y), induce: 32 (over x, z_hi, core).
Axes of the slice: x: 4, y: 4, z: 16 (z_hi: 4, z_lo: 4; z = z_hi * 4 + z_lo), core: 2. Of those that a mesh axis runs over, the one named last changes fastest.
Arguments:
- train_coords: float32 [1024, 192], P('train'), may hold values from -0.3 to 4.8, as said below
- induce_coords: float32 [4096, 192], P('induce'), may hold values from -0.3 to 4.8, as said below
- train_forces: float32 [1024, 192], P('train'), may hold values from -18 to 18
- atom_pairs: int32 [2, 2016], replicated, may hold values from 0 to 63, as said below
- length_scale: float32 [1], replicated, may hold values from 1.5 to 3
Outputs:
- coefficients: float32 [4096, 192], P('induce')
- residual: float32 [4096, 192], P('induce')
- desc_coeffs: float32 [4096, 2016], P('induce')
Inputs may be any that keep to these rules, and one draw needn't show every extreme that they name: `atom_pairs`: every unordered pair of two different atoms of the 64 stands in exactly one column, in either order. `train_coords`: atom a lies within 0.3 of 1.5 * (a % 4, a // 4 % 4, a // 16) in each component. `induce_coords`: atom a lies within 0.3 of 1.5 * (a % 4, a // 4 % 4, a // 16) in each component.
All inputs are finite; a program needn't handle non-finite values.
Results may differ from a plain program's by a relative error of at most 0.0085.
Values sent between devices are 32-bit elements; how exact they have to be, the bound alone decides.
A program may use at most 64 MiB of HBM per device.

v0:
```python
import math

import jax
import jax.numpy as jnp
from jax import lax
from jax.sharding import PartitionSpec as P

root_five = math.sqrt(5.0)


def from_everyone(value, axis):
    length = lax.axis_size(axis)
    return lax.all_to_all(
        jnp.broadcast_to(value[None], (length, *value.shape)), axis, 0, 0, tiled=True
    )


def in_order(blocks, dim):
    blocks = jnp.moveaxis(blocks, 0, dim)
    lengths = blocks.shape
    return blocks.reshape(*lengths[:dim], lengths[dim] * lengths[dim + 1], *lengths[dim + 2 :])


def gathered_copies(value, axis, dim):
    blocks = from_everyone(value, axis)
    return in_order(blocks, dim)


def split_up(value, dim, length):
    lengths = value.shape
    blocks = value.reshape(*lengths[:dim], length, lengths[dim] // length, *lengths[dim + 1 :])
    return jnp.moveaxis(blocks, dim, 0)


def sum_at_owner(value, axis, dim):
    blocks = split_up(value, dim, lax.axis_size(axis))
    arrived = lax.all_to_all(blocks, axis, split_axis=0, concat_axis=0, tiled=True)
    return arrived.sum(axis=0)


def taken_together(value, axis):
    everything = from_everyone(value, axis)
    return jnp.sum(everything, axis=0)


def sent_together(arrays, axis, dim, along):
    ends, at = ([], 0)
    for a in arrays[:-1]:
        at += a.shape[along]
        ends.append(at)
    both = jnp.concatenate(arrays, axis=along)
    return tuple(jnp.split(lax.all_gather(both, axis, axis=dim, tiled=True), ends, axis=along))


def make_incidence(atom_pairs, atom_count):
    atom_ids = jnp.arange(atom_count, dtype=jnp.int32)
    head_hit = (atom_pairs[0][:, None] == atom_ids[None, :]).astype(jnp.float32)
    tail_hit = (atom_pairs[1][:, None] == atom_ids[None, :]).astype(jnp.float32)
    return head_hit - tail_hit


def lattice_coords(atom_count):
    atom_ids = jnp.arange(atom_count, dtype=jnp.int32)
    lattice = jnp.stack([atom_ids % 4, atom_ids // 4 % 4, atom_ids // 16]).astype(jnp.float32)
    return (1.5 * lattice).reshape(1, 3 * atom_count)


def describe(coords, incidence):
    atom_count = incidence.shape[1]
    spatial = coords.reshape(coords.shape[0], 3, atom_count)
    offsets = jnp.einsum("bca,pa->bcp", spatial, incidence, precision=lax.Precision.HIGHEST)
    length = jnp.sqrt(jnp.sum(offsets * offsets, axis=1))
    return (1.0 / length, offsets / (length**3)[:, None, :])


def centered(coords, incidence):
    values, gradients = describe(coords, incidence)
    lattice_values = describe(lattice_coords(incidence.shape[1]), incidence)[0]
    return ((values - lattice_values).astype(jnp.bfloat16), gradients)


def to_desc(gradients, vectors, incidence):
    atom_count = incidence.shape[1]
    shifted = jnp.einsum(
        "bca,pa->bcp",
        vectors.reshape(vectors.shape[0], 3, atom_count),
        incidence,
        precision=lax.Precision.HIGHEST,
    )
    return -jnp.sum(gradients * shifted, axis=1)


def to_forces(gradients, values, incidence):
    weighted = gradients * values[:, None, :]
    summed = jnp.einsum("bcp,pa->bca", weighted, incidence, precision=lax.Precision.HIGHEST)
    return -summed.reshape(values.shape[0], -1)


def matern(row_desc, col_desc, length):
    inner_prod = jnp.dot(row_desc, col_desc.T, preferred_element_type=jnp.float32)
    row_sq = jnp.sum(jnp.square(row_desc.astype(jnp.float32)), axis=1)
    col_sq = jnp.sum(jnp.square(col_desc.astype(jnp.float32)), axis=1)
    radius = jnp.sqrt(row_sq[:, None] + col_sq[None, :] - 2.0 * inner_prod) / length
    falloff = jnp.exp(-root_five * radius)
    diag_part = 5.0 / (3.0 * length**2) * (1.0 + root_five * radius) * falloff
    outer_part = 25.0 / (3.0 * length**4) * falloff
    return (diag_part, outer_part)


def apply_forward(train_desc, induce_desc, diag_part, outer_part, induce_vals):
    self_dot = jnp.sum(induce_desc.astype(jnp.float32) * induce_vals.astype(jnp.float32), axis=1)
    projected = (
        jnp.dot(train_desc, induce_vals.T, preferred_element_type=jnp.float32) - self_dot[None, :]
    )
    product = outer_part * projected
    result = jnp.dot(
        diag_part.astype(jnp.bfloat16), induce_vals, preferred_element_type=jnp.float32
    )
    result = result + jnp.dot(
        product.astype(jnp.bfloat16), induce_desc, preferred_element_type=jnp.float32
    )
    return result - train_desc.astype(jnp.float32) * jnp.sum(product, axis=1)[:, None]


def apply_adjoint(train_desc, induce_desc, diag_part, outer_part, train_vals):
    self_dot = jnp.sum(train_desc.astype(jnp.float32) * train_vals.astype(jnp.float32), axis=1)
    projected = self_dot[:, None] - jnp.dot(
        train_vals, induce_desc.T, preferred_element_type=jnp.float32
    )
    product = outer_part * projected
    result = jnp.dot(
        diag_part.astype(jnp.bfloat16).T, train_vals, preferred_element_type=jnp.float32
    )
    result = result - jnp.dot(
        product.astype(jnp.bfloat16).T, train_desc, preferred_element_type=jnp.float32
    )
    return result + induce_desc.astype(jnp.float32) * jnp.sum(product, axis=0)[:, None]


def per_device(train_coords, induce_coords, train_forces, atom_pairs, length_scale):
    atom_count = train_coords.shape[1] // 3
    incidence = make_incidence(atom_pairs, atom_count)
    train_desc, train_grad = centered(train_coords, incidence)
    induce_desc, induce_grad = centered(induce_coords, incidence)
    diag_part, outer_part = matern(train_desc, induce_desc, length_scale[0])

    def forward(vectors):
        vectors = gathered_copies(vectors, "train", 0)
        induce_vals = to_desc(induce_grad, vectors, incidence).astype(jnp.bfloat16)
        partial_forces = to_forces(
            train_grad,
            apply_forward(train_desc, induce_desc, diag_part, outer_part, induce_vals),
            incidence,
        )
        summed = sum_at_owner(partial_forces, "induce", 0)
        return gathered_copies(summed, "induce", 0)

    def adjoint(forces_like):
        train_vals = to_desc(train_grad, forces_like, incidence).astype(jnp.bfloat16)
        partial_coeffs = to_forces(
            induce_grad,
            apply_adjoint(train_desc, induce_desc, diag_part, outer_part, train_vals),
            incidence,
        )
        return sum_at_owner(partial_coeffs, "train", 0)

    start = adjoint(train_forces)
    probed = forward(start)
    probed_local = jnp.sum(probed * probed)
    cross_local = jnp.sum(train_forces * probed)
    probed_sq = taken_together(probed_local, "train")
    cross_sq = taken_together(cross_local, "train")
    quotient = probed_sq / cross_sq
    center = 0.775 * quotient
    spread = 0.725 * quotient
    momentum = spread / center
    direction = start / center
    coefficients = direction
    residual = start - adjoint(probed) / center
    momentum_next = 1.0 / (2.0 * center / spread - momentum)
    direction = momentum_next * momentum * direction + 2.0 * momentum_next / spread * residual
    coefficients = coefficients + direction
    residual = residual - adjoint(forward(direction))
    coefficients, residual = sent_together((coefficients, residual), "train", 0, 1)
    desc_coeffs = to_desc(induce_grad, coefficients, incidence)
    return (coefficients, residual, desc_coeffs)


def solution(mesh):
    in_specs = (P("train", None), P("induce", None), P("train", None), P(), P())
    out_specs = (P("induce", None), P("induce", None), P("induce", None))
    return jax.shard_map(
        per_device, mesh=mesh, in_specs=in_specs, out_specs=out_specs, check_vma=False
    )
```

profile of v0, /device:TPU:2, one launch (start us, length us, event | category | flops | bytes accessed | tf_op | source)
XLA Modules:
  0.0 280.9 jit_solution(3959026815836857699)
XLA Ops:
  1.4 0.8 fusion.126
  2.2 0.5 fusion.46
  2.7 0.9 copy.57
  3.6 0.9 copy.59
  4.5 1.5 multiply_reduce_fusion.3
  6.2 4.5 %fusion = (f32[128,2016]{0,1:T(8,128)S(1)}, f32[2016,128,3]{1,0,2:T(8,128)}) fusion(f32[128,3,64]{0,2,1:T(8,128)S(1)} %bitcast.95, s32[2016]{0:T(1024)S(1)} %bitcast.115, s32[2016]{0:T(1024)S(1)} %bitcast.101), kind=kOutput, calls=%fused_computation.2 | convolution fusion | flops 596477952 | bytes 4243200 | tf_op jit(solution)/shard_map/bca,pa->bcp/dot_general | solution.py:71
  10.8 1.6 fusion.20
  12.7 0.5 fusion.47
  13.5 0.4 fusion.120
  14.1 0.4 fusion.10
  14.5 1.2 copy-done.1
  15.7 2.3 fusion.29
  18.4 17.4 %all_to_all.57 = f32[16,8,192]{2,1,0:T(8,128)S(1)} all-to-all(f32[16,8,192]{2,1,0:T(8,128)S(1)} %neg.55), channel_id=1, replica_groups=mesh['train'=16,'induce'=32] {'train'}, dimensions={0} | all-to-all | bytes 196608 | tf_op jit(solution)/shard_map/all_to_all | solution.py:37
  35.8 11.8 %all_to_all.58 = f32[16,8,192]{2,1,0:T(8,128)S(1)} all-to-all(f32[16,8,192]{2,1,0:T(8,128)S(1)} %broadcast_in_dim.12), channel_id=1, replica_groups=mesh['train'=16,'induce'=32] {'train'}, dimensions={0} | all-to-all | bytes 196608 | tf_op jit(solution)/shard_map/all_to_all | solution.py:13
  47.7 5.3 %multiply_reduce_fusion.2 = f32[128,2016]{0,1:T(8,128)S(1)} fusion(s32[2016]{0:T(1024)S(1)} %bitcast.118, s32[2016]{0:T(1024)S(1)} %bitcast.104, f32[128,3,64]{2,1,0:T(4,128)S(1)} %reshape_reshape.14, f32[128,2016]{0,1:T(8,128)S(1)} %get-tuple-element.19, f32[2016,128,3]{1,0,2:T(8,128)} %get-tuple-element.27), kind=kOutput, calls=%fused_computation.9 | convolution fusion | flops 597252096 | bytes 5275392 | tf_op jit(solution)/shard_map/bca,pa->bcp/dot_general | solution.py:84
  54.5 1.5 fusion.23
  56.2 28.9 %all_to_all.59 = f32[32,2,192]{2,1,0:T(2,128)S(1)} all-to-all(f32[32,2,192]{2,1,0:T(2,128)S(1)} %neg.58), channel_id=1, replica_groups=mesh['train'=16,'induce'=32] {'induce'}, dimensions={0} | all-to-all | bytes 98304 | tf_op jit(solution)/shard_map/all_to_all | solution.py:37
  85.2 18.2 %all_to_all.60 = f32[32,2,192]{2,1,0:T(2,128)S(1)} all-to-all(f32[32,2,192]{2,1,0:T(2,128)S(1)} %broadcast_in_dim.13), channel_id=1, replica_groups=mesh['train'=16,'induce'=32] {'induce'}, dimensions={0} | all-to-all | bytes 98304 | tf_op jit(solution)/shard_map/all_to_all | solution.py:13
  103.5 3.0 %fusion.21 = f32[64,2016]{1,0:T(8,128)S(1)} fusion(s32[2016]{0:T(1024)S(1)} %bitcast.120, s32[2016]{0:T(1024)S(1)} %bitcast.106, f32[64,3,64]{2,1,0:T(4,128)S(1)} %reshape_reshape.15, f32[64,3,2016]{2,0,1:T(8,128)} %copy-done.3, f32[64,2016]{1,0:T(8,128)S(1)} %copy-done.9), kind=kOutput, calls=%fused_computation.44 | convolution fusion | flops 298948608 | bytes 2645760 | tf_op jit(solution)/shard_map/bca,pa->bcp/dot_general | solution.py:84
  107.1 0.7 multiply_reduce_fusion.5
  107.8 1.2 broadcast_in_dim.14
  109.0 4.5 %all-to-all-start.4 = ((f32[16,1,1]{2,1,0:T(1,128)}), f32[16,1,1]{2,1,0:T(1,128)S(1)}, u32[]{:S(2)}, u32[]{:S(2)}) async-start(f32[16,1,1]{2,1,0:T(1,128)} %broadcast_in_dim.14), calls=%async_computation.4 | async-start | bytes 16384 | tf_op jit(solution)/shard_map/all_to_all | solution.py:13
  113.8 0.4 fusion.9
  114.2 0.6 multiply_reduce_fusion.4
  114.9 6.5 %all-to-all-done.4 = f32[16,1,1]{2,1,0:T(1,128)S(1)} async-done(((f32[16,1,1]{2,1,0:T(1,128)}), f32[16,1,1]{2,1,0:T(1,128)S(1)}, u32[]{:S(2)}, u32[]{:S(2)}) %all-to-all-start.4) | async-done | bytes 96 | tf_op jit(solution)/shard_map/all_to_all | solution.py:13
  121.4 1.2 broadcast_in_dim.15
  122.6 3.5 %all-to-all-start.5 = ((f32[16,1,1]{2,1,0:T(1,128)}), f32[16,1,1]{2,1,0:T(1,128)S(1)}, u32[]{:S(2)}, u32[]{:S(2)}) async-start(f32[16,1,1]{2,1,0:T(1,128)} %broadcast_in_dim.15), calls=%async_computation.5 | async-start | bytes 16384 | tf_op jit(solution)/shard_map/all_to_all | solution.py:13
  126.1 4.5 %fusion.32 = f32[128,3,64]{0,2,1:T(8,128)S(1)} fusion(f32[128,2016]{0,1:T(8,128)S(1)} %fusion.9, s32[2016]{0:T(1024)S(1)} %bitcast.121, s32[2016]{0:T(1024)S(1)} %bitcast.107, f32[2016,128,3]{1,0,2:T(8,128)} %get-tuple-element.27, f32[128,2016]{0,1:T(8,128)} %copy-done.6), kind=kOutput, calls=%fused_computation.55 | convolution fusion | flops 596760576 | bytes 5275392 | tf_op jit(solution)/shard_map/bcp,pa->bca/dot_general | solution.py:95
  130.7 0.9 neg.61
  131.6 2.3 all-to-all-done.5
  133.9 5.2 %all-to-all-start.6 = ((f32[16,8,192]{2,1,0:T(8,128)}), f32[16,8,192]{2,1,0:T(8,128)S(1)}, u32[]{:S(2)}, u32[]{:S(2)}) async-start(f32[16,8,192]{2,1,0:T(8,128)} %neg.61), calls=%async_computation.6 | async-start | bytes 262144 | tf_op jit(solution)/shard_map/all_to_all | solution.py:37
  139.1 0.6 reduce_sum.288
  139.7 0.6 reduce_sum.290
  141.8 6.2 %all-to-all-done.6 = f32[16,8,192]{2,1,0:T(8,128)S(1)} async-done(((f32[16,8,192]{2,1,0:T(8,128)}), f32[16,8,192]{2,1,0:T(8,128)S(1)}, u32[]{:S(2)}, u32[]{:S(2)}) %all-to-all-start.6) | async-done | bytes 98336 | tf_op jit(solution)/shard_map/all_to_all | solution.py:37
  148.1 20.7 %all_to_all.61 = f32[16,8,192]{2,1,0:T(8,128)S(1)} all-to-all(f32[16,8,192]{2,1,0:T(8,128)S(1)} %broadcast_in_dim.16), channel_id=1, replica_groups=mesh['train'=16,'induce'=32] {'train'}, dimensions={0} | all-to-all | bytes 196608 | tf_op jit(solution)/shard_map/all_to_all | solution.py:13
  168.9 5.5 %multiply_reduce_fusion.1 = f32[128,2016]{0,1:T(8,128)S(1)} fusion(s32[2016]{0:T(1024)S(1)} %bitcast.122, s32[2016]{0:T(1024)S(1)} %bitcast.108, f32[128,3,64]{2,1,0:T(4,128)S(1)} %reshape_reshape.16, f32[128,2016]{0,1:T(8,128)} %copy-done.6, f32[2016,128,3]{1,0,2:T(8,128)} %get-tuple-element.27), kind=kOutput, calls=%fused_computation.6 | convolution fusion | flops 597252096 | bytes 5275392 | tf_op jit(solution)/shard_map/bca,pa->bcp/dot_general | solution.py:84
  175.9 1.5 fusion.26
  177.6 18.3 %all_to_all.62 = f32[32,2,192]{2,1,0:T(2,128)S(1)} all-to-all(f32[32,2,192]{2,1,0:T(2,128)S(1)} %neg.64), channel_id=1, replica_groups=mesh['train'=16,'induce'=32] {'induce'}, dimensions={0} | all-to-all | bytes 98304 | tf_op jit(solution)/shard_map/all_to_all | solution.py:37
  196.0 18.2 %all_to_all.63 = f32[32,2,192]{2,1,0:T(2,128)S(1)} all-to-all(f32[32,2,192]{2,1,0:T(2,128)S(1)} %broadcast_in_dim.17), channel_id=1, replica_groups=mesh['train'=16,'induce'=32] {'induce'}, dimensions={0} | all-to-all | bytes 98304 | tf_op jit(solution)/shard_map/all_to_all | solution.py:13
  214.4 1.5 fusion.22
  216.7 0.4 fusion.8
  217.2 0.6 copy-done.2
  218.1 2.3 fusion.35
  220.7 13.4 %all_to_all.64 = f32[16,8,192]{2,1,0:T(8,128)S(1)} all-to-all(f32[16,8,192]{2,1,0:T(8,128)S(1)} %neg.67), channel_id=1, replica_groups=mesh['train'=16,'induce'=32] {'train'}, dimensions={0} | all-to-all | bytes 196608 | tf_op jit(solution)/shard_map/all_to_all | solution.py:37
  234.3 39.2 %all_gather.3 = f32[128,384]{1,0:T(8,128)S(1)} all-gather(f32[8,384]{1,0:T(8,128)S(1)} %pad_maximum_fusion), channel_id=1, replica_groups=mesh['train'=16,'induce'=32] {'train'}, dimensions={0}, use_global_device_ids=true | all-gather | bytes 208896 | tf_op jit(solution)/shard_map/all_gather | solution.py:52
  273.6 0.7 copy.74
  274.4 5.3 %multiply_reduce_fusion = f32[128,2016]{0,1:T(8,128)S(1)} fusion(f32[128,3,64]{0,2,1:T(8,128)S(1)} %bitcast.97, s32[2016]{0:T(1024)S(1)} %bitcast.126, s32[2016]{0:T(1024)S(1)} %bitcast.112, f32[128,2016]{0,1:T(8,128)S(1)} %copy-done.7, f32[2016,128,3]{1,0,2:T(8,128)} %get-tuple-element.27), kind=kOutput, calls=%fused_computation.3 | convolution fusion | flops 597252096 | bytes 5275392 | tf_op jit(solution)/shard_map/bca,pa->bcp/dot_general | solution.py:84
  279.7 1.0 neg.68
  (73 shorter events, 8.1 us)
Async XLA Ops:
  0.6 5.6 %copy-start = (f32[128,192]{0,1:T(8,128)S(1)}, f32[128,192]{0,1:T(8,128)}, u32[]{:S(2)}) copy-start(f32[128,192]{0,1:T(8,128)} %param.6) | copy-start | bytes 294916
  6.0 6.4 %copy-start.3 = (f32[64,3,2016]{2,0,1:T(8,128)}, f32[64,3,2016]{2,0,1:T(8,128)S(1)}, u32[]{:S(2)}) copy-start(f32[64,3,2016]{2,0,1:T(8,128)S(1)} %get-tuple-element.25) | copy-start | bytes 4644868
  6.2 6.2 %copy-start.8 = (f32[64,2016]{1,0:T(8,128)}, f32[64,2016]{1,0:T(8,128)S(1)}, u32[]{:S(2)}) copy-start(f32[64,2016]{1,0:T(8,128)S(1)} %multiply_multiply_fusion.1) | copy-start | bytes 1548292
  13.1 34.5 %copy-start.6 = (f32[128,2016]{0,1:T(8,128)}, f32[128,2016]{0,1:T(8,128)S(1)}, u32[]{:S(2)}) copy-start(f32[128,2016]{0,1:T(8,128)S(1)} %get-tuple-element.19) | copy-start | bytes 3096580
  13.9 1.9 copy-start.1
  53.0 1.4 copy-start.4
  53.0 1.5 copy-start.9
  106.5 7.7 %copy-start.11 = (f32[64,192]{1,0:T(8,128)S(1)}, f32[64,192]{1,0:T(8,128)}, u32[]{:S(2)}) copy-start(f32[64,192]{1,0:T(8,128)} %param.7) | copy-start | bytes 147460
  109.0 12.3 %all-to-all-start.4 = ((f32[16,1,1]{2,1,0:T(1,128)}), f32[16,1,1]{2,1,0:T(1,128)S(1)}, u32[]{:S(2)}, u32[]{:S(2)}) async-start(f32[16,1,1]{2,1,0:T(1,128)} %broadcast_in_dim.14), calls=%async_computation.4 | async-start | bytes 16384 | tf_op jit(solution)/shard_map/all_to_all | solution.py:13
  122.6 11.3 %all-to-all-start.5 = ((f32[16,1,1]{2,1,0:T(1,128)}), f32[16,1,1]{2,1,0:T(1,128)S(1)}, u32[]{:S(2)}, u32[]{:S(2)}) async-start(f32[16,1,1]{2,1,0:T(1,128)} %broadcast_in_dim.15), calls=%async_computation.5 | async-start | bytes 16384 | tf_op jit(solution)/shard_map/all_to_all | solution.py:13
  133.9 14.1 %all-to-all-start.6 = ((f32[16,8,192]{2,1,0:T(8,128)}), f32[16,8,192]{2,1,0:T(8,128)S(1)}, u32[]{:S(2)}, u32[]{:S(2)}) async-start(f32[16,8,192]{2,1,0:T(8,128)} %neg.61), calls=%async_computation.6 | async-start | bytes 262144 | tf_op jit(solution)/shard_map/all_to_all | solution.py:37
  174.4 1.4 copy-start.5
  174.4 1.5 copy-start.10
  215.9 1.9 copy-start.2
  215.9 2.1 copy-start.7
  274.4 5.3 %copy-start.12 = (f32[128,192]{0,1:T(8,128)}, f32[128,192]{0,1:T(8,128)S(1)}, u32[]{:S(2)}) copy-start(f32[128,192]{0,1:T(8,128)S(1)} %copy.73) | copy-start | bytes 294916
where the time goes:
time: 285 us; the launch traced here: 281 us
  blocking collectives  186 us (65%)
  matrix products  46.2 us (16%)
  waiting for transfers between devices  14.9 us (5%)
  starting transfers between devices  13.2 us (5%)
  local copies, waits for them, and re-layouts  11.3 us (4%)
  other arithmetic  5.68 us (2%)
  between operations  3.53 us (1%)
    all_to_all x4, blocking collectives, sum_at_owner(): lax.all_to_all(blocks, axis, split_axis=0, concat_axis=0, tiled=True)  78 us
    all_to_all x4, blocking collectives, from_everyone(): lax.all_to_all(jnp.broadcast_to(value[None], (length, *value.shape)), axi...  68.9 us
    all_gather x1, blocking collectives, sent_together(): lax.all_gather(both, axis, axis=dim, tiled=True)  39.2 us
    dot_general x6, matrix products, to_desc(): jnp.einsum('bca,pa->bcp', vectors.reshape(vectors.shape[0], 3, atom_count...  22.2 us
    dot_general x5, matrix products, to_forces(): jnp.einsum('bcp,pa->bca', weighted, incidence, precision=lax.Precision.HI...  12.1 us
    all_to_all x2, waiting for transfers between devices, from_everyone(): lax.all_to_all(jnp.broadcast_to(value[None], (length, *value.shape)), axi...  8.76 us
    all_to_all x2, starting transfers between devices, from_everyone(): lax.all_to_all(jnp.broadcast_to(value[None], (length, *value.shape)), axi...  7.96 us
    dot_general x3, matrix products, describe(): jnp.einsum('bca,pa->bcp', spatial, incidence, precision=lax.Precision.HIG...  6.52 us
  transfers between devices with their start and end apart: 3, of which 3 were waited for; matrix products, arithmetic and copies ran while one was open for 3% of the time, Pallas kernels for 0%

commit v1 on v0

v1 whole, which is shorter than its diff:
```python
import functools
import math

import jax
import jax.numpy as jnp
from jax import lax
from jax.experimental import pallas as pl
from jax.experimental.pallas import tpu as pltpu
from jax.sharding import PartitionSpec as P

MESH = pl.DeviceIdType.MESH
F32, BF16 = jnp.float32, jnp.bfloat16
ROOT5 = math.sqrt(5.0)
ATOMS, DESC, PAD = 64, 2016, 2048
NT, NI = 64, 128
TILE = 512
TILES = [pl.ds(j * TILE, TILE) for j in range(PAD // TILE)]
N_TRAIN, N_OWN = 16, 8
OWN0 = 4
N_PLANE, P_OWN = 8, 6
N_ZHI = 4


def dot(a, b):
    return jnp.dot(a, b, preferred_element_type=F32)


def dot_nt(a, b):
    return lax.dot_general(a, b, (((1,), (1,)), ((), ())), preferred_element_type=F32)


def lane_of(shape):
    return lax.broadcasted_iota(jnp.int32, shape, len(shape) - 1)


def pack(wide):
    half = wide.shape[0] // 2
    left = wide[:, 0:128]
    right = jnp.concatenate([wide[:, 128:192], jnp.zeros((wide.shape[0], 64), F32)], axis=1)
    left_turned, right_turned = pltpu.roll(left, 64, 1), pltpu.roll(right, 64, 1)
    low = lane_of((half, 128)) < 64
    return [
        jnp.where(low, left[:half], left_turned[half:]),
        jnp.where(low, left_turned[:half], left[half:]),
        jnp.where(low, right[:half], right_turned[half:]),
    ]


def unpack_into(ref, planes):
    half = planes[0].shape[0]
    low = lane_of((half, 128)) < 64
    turned = [pltpu.roll(p, 64, 1) for p in planes]
    ref[0:half, 0:128] = jnp.where(low, planes[0], turned[1])
    ref[half : 2 * half, 0:128] = jnp.where(low, turned[0], planes[1])
    ref[0:half, 128:192] = planes[2][:, 0:64]
    ref[half : 2 * half, 128:192] = turned[2][:, 0:64]


def two_parts(full):
    high = full.astype(BF16)
    low = (full - high.astype(F32)).astype(BF16)
    return jnp.concatenate([high, low], axis=1)


def spread(planes):
    rows = []
    for plane in planes:
        low = lane_of(plane.shape) < 64
        rows.append(jnp.where(low, plane, 0.0))
        rows.append(jnp.where(low, 0.0, plane))
    return two_parts(jnp.concatenate(rows, axis=0))


def kernel(
    tc, ic, tf, pairs, scale,
    out_coeff, out_resid, out_desc,
    ends, inc, inc_t, grad_t, grad_i, z, vu, vw, desc,
    s_part0, s_part1, s_part2, s_in0, s_in1, s_in2, s_all0, s_all1, s_all2,
    p_part0, p_part1, p_in0, p_in1, p_z0, p_z1, p_all0, p_all1,
    rs_send, rs_recv, ag_send, ag_recv,
    pr_send, pr_recv, pz_send, pz_recv, pg_send, pg_recv, desc_sem,
):
    s_part, s_in, s_all = [s_part0, s_part1, s_part2], [s_in0, s_in1, s_in2], [s_all0, s_all1, s_all2]
    p_part, p_in, p_z, p_all = [p_part0, p_part1], [p_in0, p_in1], [p_z0, p_z1], [p_all0, p_all1]
    t = lax.axis_index("train")
    i = lax.axis_index("induce")
    x, zh, core = i // 8, (i // 2) % 4, i % 2
    spot = x * 2 + core

    def in_plane(other):
        return (t, (other // 2) * 8 + zh * 2 + other % 2)

    def in_column(other):
        return (t, x * 8 + other * 2 + core)

    barrier = pltpu.get_barrier_semaphore()
    for d in range(1, N_TRAIN):
        pl.semaphore_signal(barrier, inc=1, device_id=(lax.rem(t + d, N_TRAIN), i), device_id_type=MESH)
    for d in range(1, N_PLANE):
        pl.semaphore_signal(barrier, inc=1, device_id=in_plane(lax.rem(spot + d, N_PLANE)), device_id_type=MESH)
    for d in range(1, N_ZHI):
        pl.semaphore_signal(barrier, inc=1, device_id=in_column(lax.rem(zh + d, N_ZHI)), device_id_type=MESH)

    ends[...] = jnp.full((2, PAD), -1, jnp.int32)
    ends[:, 0:DESC] = pairs[...]
    atom = lax.rem(lax.broadcasted_iota(jnp.int32, (128, PAD), 0), ATOMS)
    hits = (ends[0:1, :] == atom).astype(F32) - (ends[1:2, :] == atom).astype(F32)
    inc[0:128, :] = hits.astype(BF16)
    inc[128:256, :] = hits.astype(BF16)
    inc_t[...] = hits.T.astype(BF16)

    spot_atom = lax.rem(lane_of((1, 128)), ATOMS)
    lattice = [
        1.5 * lax.rem(spot_atom, 4).astype(F32),
        1.5 * lax.rem(spot_atom // 4, 4).astype(F32),
        1.5 * (spot_atom // 16).astype(F32),
    ]

    def coordinate_rows(planes):
        high, low = [], []
        for plane, points in zip(planes, lattice):
            offset = plane - points
            first = lane_of(plane.shape) < 64
            top = offset.astype(BF16).astype(F32)
            rest = offset - top
            full = jnp.broadcast_to(points, plane.shape)
            high += [jnp.where(first, top, full), jnp.where(first, full, top)]
            low += [jnp.where(first, rest, 0.0), jnp.where(first, 0.0, rest)]
        return jnp.concatenate(
            [jnp.concatenate(high, axis=0).astype(BF16), jnp.concatenate(low, axis=0).astype(BF16)], axis=1
        )

    first8 = lane_of((8, 128)) < 64
    lattice_rows = jnp.concatenate(
        [jnp.where(first8, jnp.broadcast_to(points, (8, 128)), 0.0) for points in lattice], axis=0
    )
    lattice_rows = jnp.concatenate([lattice_rows, jnp.zeros((24, 128), F32)], axis=1).astype(BF16)
    rows_t, rows_i = coordinate_rows(pack(tc[...])), coordinate_rows(pack(ic[...]))

    def describe(rows, tile, last):
        n = rows.shape[0] // 3
        off = dot(rows, inc[:, tile])
        off = [off[0:n], off[n : 2 * n], off[2 * n :]]
        square = off[0] * off[0] + off[1] * off[1] + off[2] * off[2]
        if last:
            square = jnp.where(lane_of(square.shape) < DESC - (PAD - TILE), square, 1.0)
        inverse = lax.rsqrt(square)
        return off, inverse

    for j, tile in enumerate(TILES):
        last = j == len(TILES) - 1
        unused, rest = describe(lattice_rows, tile, last)
        for rows, grad, at, n in ((rows_t, grad_t, 0, NT), (rows_i, grad_i, NT, NI)):
            off, inverse = describe(rows, tile, last)
            cube = -(inverse * inverse * inverse)
            for c in range(3):
                grad[c, :, tile] = off[c] * cube
            z[at : at + n, tile] = (inverse - rest[0:1]).astype(BF16)
    vu[NI:, :] = z[NT:, :]
    vw[NT:, :] = z[0:NT, :]

    length = scale[0]
    gram_t = dot_nt(z[...], z[0:NT, :])
    gram_i = dot_nt(z[...], z[NT:, :])

    def on_diagonal(square, axis):
        rows, columns = square.shape
        same = lax.broadcasted_iota(jnp.int32, (rows, columns), 0) == lane_of((rows, columns))
        return jnp.sum(jnp.where(same, square, 0.0), axis=axis, keepdims=True)

    def matern(inner, row_sq, col_sq):
        radius = jnp.sqrt(jnp.maximum(row_sq + col_sq - 2.0 * inner, 0.0)) / length
        falloff = jnp.exp(-ROOT5 * radius)
        return (
            5.0 / (3.0 * (length * length)) * (1.0 + ROOT5 * radius) * falloff,
            25.0 / (3.0 * (length * length) * (length * length)) * falloff,
        )

    diag, outer = matern(gram_i[0:NT], on_diagonal(gram_t[0:NT], 1), on_diagonal(gram_i[NT:], 0))
    diag_back, outer_back = matern(gram_t[NT:], on_diagonal(gram_i[NT:], 1), on_diagonal(gram_t[0:NT], 0))
    diag = diag.astype(BF16)
    diag_back = jnp.concatenate([diag_back, jnp.zeros((NI, 64), F32)], axis=1)
    outer_back = pltpu.roll(jnp.concatenate([outer_back, jnp.zeros((NI, 64), F32)], axis=1), 64, 1)

    def to_desc(rows, grad, tile):
        n = grad.shape[1]
        moved = dot(rows, inc[:, tile])
        return grad[0, :, tile] * moved[0:n] + grad[1, :, tile] * moved[n : 2 * n] + grad[2, :, tile] * moved[2 * n :]

    def to_forces(values, grad, tile):
        weighted = [(grad[c, :, tile] * values).astype(BF16) for c in range(3)]
        return dot(jnp.concatenate(weighted, axis=0), inc_t[tile, :])

    def packed_planes(total):
        n = total.shape[0] // 3
        low = lane_of((n // 2, 128)) < 64
        return [
            jnp.where(low, total[c * n : c * n + n // 2], total[c * n + n // 2 : (c + 1) * n]) for c in range(3)
        ]

    def forward(planes):
        rows = spread(planes)
        for tile in TILES:
            vu[0:NI, tile] = to_desc(rows, grad_i, tile).astype(BF16)
        gram = dot_nt(z[...], vu[0:NI, :])
        product = outer * (gram[0:NT] - on_diagonal(gram[NT:], 0))
        row_sum = jnp.sum(product, axis=1, keepdims=True)
        both = jnp.concatenate([diag, product.astype(BF16)], axis=1)
        total = jnp.zeros((3 * NT, 128), F32)
        for tile in TILES:
            w = dot(both, vu[:, tile]) - z[0:NT, tile].astype(F32) * row_sum
            total = total + to_forces(w, grad_t, tile)
        return packed_planes(total)

    def adjoint(planes):
        rows = spread(planes)
        for tile in TILES:
            vw[0:NT, tile] = to_desc(rows, grad_t, tile).astype(BF16)
        gram = pltpu.roll(dot_nt(z[...], vw[...]), 64, 1)
        same = lax.broadcasted_iota(jnp.int32, (NT, 128), 0) + 64 == lane_of((NT, 128))
        self_dot = jnp.sum(jnp.where(same, gram[0:NT], 0.0), axis=0, keepdims=True)
        product = outer_back * (self_dot - gram[NT:])
        col_sum = jnp.sum(product, axis=1, keepdims=True)
        both = jnp.where(lane_of((NI, 128)) < 64, diag_back, -product).astype(BF16)
        total = jnp.zeros((3 * NI, 128), F32)
        for tile in TILES:
            h = dot(both, vw[:, tile]) + z[NT:, tile].astype(F32) * col_sum
            total = total + to_forces(h, grad_i, tile)
        return packed_planes(total)

    is_owner = jnp.logical_and(t >= OWN0, t < OWN0 + N_OWN)
    mine = lax.rem(t + N_OWN - OWN0, N_OWN)
    waits = []

    def chunk_rows(k):
        return pl.ds(pl.multiple_of(k * 8, 8), 8)

    def sum_over_train(n, planes, extra=None):
        part, arrived, everything = s_part[n], s_in[n], s_all[n]
        for c in range(3):
            part[c] = planes[c]
        if extra is not None:
            for k in range(N_OWN):
                part[3, k * 8 : (k + 1) * 8, :] = extra

        def scatter(d):
            k = lax.rem(mine + d, N_OWN)
            return pltpu.make_async_remote_copy(
                src_ref=part.at[:, chunk_rows(k), :], dst_ref=arrived.at[t],
                send_sem=rs_send.at[n, d], recv_sem=rs_recv.at[n, t],
                device_id=(k + OWN0, i), device_id_type=MESH,
            )

        def gather(d):
            return pltpu.make_async_remote_copy(
                src_ref=everything.at[:, chunk_rows(mine), :], dst_ref=everything.at[:, chunk_rows(mine), :],
                send_sem=ag_send.at[n, d], recv_sem=ag_recv.at[n, mine],
                device_id=(lax.rem(t + d, N_TRAIN), i), device_id_type=MESH,
            )

        for d in range(1, N_OWN):
            scatter(d).start()

        @pl.when(jnp.logical_not(is_owner))
        def _():
            scatter(0).start()

        @pl.when(is_owner)
        def _():
            total = part[:, chunk_rows(mine), :]
            for d in range(1, N_TRAIN):
                source = lax.rem(t + d, N_TRAIN)
                pltpu.make_async_remote_copy(
                    src_ref=part.at[:, chunk_rows(mine), :], dst_ref=arrived.at[source],
                    send_sem=rs_send.at[n, 0], recv_sem=rs_recv.at[n, source],
                    device_id=(source, i), device_id_type=MESH,
                ).wait_recv()
                total = total + arrived[source]
            everything[:, chunk_rows(mine), :] = total
            for d in range(1, N_TRAIN):
                gather(d).start()

        def arrive():
            for k in range(N_OWN):
                @pl.when(t != k + OWN0)
                def _():
                    rows = pl.ds(k * 8, 8)
                    pltpu.make_async_remote_copy(
                        src_ref=everything.at[:, rows, :], dst_ref=everything.at[:, rows, :],
                        send_sem=ag_send.at[n, 0], recv_sem=ag_recv.at[n, k],
                        device_id=(k + OWN0, i), device_id_type=MESH,
                    ).wait_recv()
            return [everything[c] for c in range(3)]

        def finish():
            for d in range(1, N_OWN):
                scatter(d).wait_send()

            @pl.when(jnp.logical_not(is_owner))
            def _():
                scatter(0).wait_send()

            @pl.when(is_owner)
            def _():
                for d in range(1, N_TRAIN):
                    gather(d).wait_send()

        waits.append(finish)
        return arrive

    has_chunk = spot < P_OWN

    def sum_over_induce(n, planes):
        part, arrived, column, everything = p_part[n], p_in[n], p_z[n], p_all[n]
        for c in range(3):
            for r in range(4):
                part[c * 4 + r] = planes[c][r * 8 : (r + 1) * 8]

        def pair_of(k):
            return pl.ds(k * 2, 2)

        def scatter(d):
            k = lax.rem(spot + d, P_OWN)
            return pltpu.make_async_remote_copy(
                src_ref=part.at[pair_of(k)], dst_ref=arrived.at[spot],
                send_sem=pr_send.at[n, d], recv_sem=pr_recv.at[n, spot],
                device_id=in_plane(k), device_id_type=MESH,
            )

        def across(d):
            return pltpu.make_async_remote_copy(
                src_ref=column.at[zh], dst_ref=column.at[zh],
                send_sem=pz_send.at[n, d], recv_sem=pz_recv.at[n, zh],
                device_id=in_column(lax.rem(zh + d, N_ZHI)), device_id_type=MESH,
            )

        def gather(d):
            return pltpu.make_async_remote_copy(
                src_ref=everything.at[pair_of(spot)], dst_ref=everything.at[pair_of(spot)],
                send_sem=pg_send.at[n, d], recv_sem=pg_recv.at[n, spot],
                device_id=in_plane(lax.rem(spot + d, N_PLANE)), device_id_type=MESH,
            )

        for d in range(1, P_OWN):
            scatter(d).start()

        @pl.when(jnp.logical_not(has_chunk))
        def _():
            scatter(0).start()

        @pl.when(has_chunk)
        def _():
            total = part[pair_of(spot)]
            for d in range(1, N_PLANE):
                source = lax.rem(spot + d, N_PLANE)
                pltpu.make_async_remote_copy(
                    src_ref=part.at[pair_of(spot)], dst_ref=arrived.at[source],
                    send_sem=pr_send.at[n, 0], recv_sem=pr_recv.at[n, source],
                    device_id=in_plane(source), device_id_type=MESH,
                ).wait_recv()
                total = total + arrived[source]
            column[zh] = total
            for d in (2, 1, 3):
                across(d).start()
            for d in range(1, N_ZHI):
                source = lax.rem(zh + d, N_ZHI)
                pltpu.make_async_remote_copy(
                    src_ref=column.at[zh], dst_ref=column.at[source],
                    send_sem=pz_send.at[n, 0], recv_sem=pz_recv.at[n, source],
                    device_id=in_column(source), device_id_type=MESH,
                ).wait_recv()
            everything[pair_of(spot)] = (column[0] + column[1]) + (column[2] + column[3])
            for d in range(1, N_PLANE):
                gather(d).start()

        def arrive():
            for k in range(P_OWN):
                @pl.when(spot != k)
                def _():
                    pltpu.make_async_remote_copy(
                        src_ref=everything.at[pair_of(k)], dst_ref=everything.at[pair_of(k)],
                        send_sem=pg_send.at[n, 0], recv_sem=pg_recv.at[n, k],
                        device_id=in_plane(k), device_id_type=MESH,
                    ).wait_recv()
            return [everything[c * 4 : (c + 1) * 4].reshape(32, 128) for c in range(3)]

        def finish():
            for d in range(1, P_OWN):
                scatter(d).wait_send()

            @pl.when(jnp.logical_not(has_chunk))
            def _():
                scatter(0).wait_send()

            @pl.when(has_chunk)
            def _():
                for d in range(1, N_ZHI):
                    across(d).wait_send()
                for d in range(1, N_PLANE):
                    gather(d).wait_send()

        waits.append(finish)
        return arrive

    def whole_sum(planes, others):
        line = sum(jnp.sum(a * b, axis=0, keepdims=True) for a, b in zip(planes, others))
        return jnp.sum(line, axis=1, keepdims=True)

    forces = pack(tf[...])
    first = adjoint(forces)
    pl.semaphore_wait(barrier, N_TRAIN - 1 + N_PLANE - 1 + N_ZHI - 1)
    start = sum_over_train(0, first)()
    probed = sum_over_induce(0, forward(start))()
    row8 = lax.broadcasted_iota(jnp.int32, (8, 128), 0)
    sums = jnp.where(row8 == 0, whole_sum(probed, probed), whole_sum(forces, probed))
    again = sum_over_train(1, adjoint(probed), sums)()
    quotient = s_all1[3, 0:1, 0:1] / s_all1[3, 1:2, 0:1]
    center = 0.775 * quotient
    spread_ = 0.725 * quotient
    momentum = spread_ / center
    following = 1.0 / (2.0 * center / spread_ - momentum)
    direction = [a / center for a in start]
    residual = [a - b / center for a, b in zip(start, again)]
    turned = [following * momentum * a + 2.0 * following / spread_ * b for a, b in zip(direction, residual)]
    coeffs = [a + b for a, b in zip(direction, turned)]
    arrive = sum_over_induce(1, forward(turned))
    unpack_into(out_coeff, coeffs)
    rows = spread(coeffs)
    for j, tile in enumerate(TILES):
        width = min(TILE, DESC - j * TILE)
        desc[:, pl.ds(j * TILE, width)] = to_desc(rows, grad_i, tile)[:, 0:width]
    copy = pltpu.make_async_copy(desc, out_desc, desc_sem)
    copy.start()
    final = sum_over_train(2, adjoint(arrive()))()
    unpack_into(out_resid, [a - b for a, b in zip(residual, final)])
    for finish in waits:
        finish()
    copy.wait()


def per_device(train_coords, induce_coords, train_forces, atom_pairs, length_scale):
    vmem, dma = pltpu.VMEM, pltpu.SemaphoreType.DMA
    whole = pl.BlockSpec(memory_space=pltpu.VMEM)
    scratch = [
        vmem((2, PAD), jnp.int32), vmem((256, PAD), BF16), vmem((PAD, 128), BF16),
        vmem((3, NT, PAD), F32), vmem((3, NI, PAD), F32),
        vmem((NT + NI, PAD), BF16), vmem((2 * NI, PAD), BF16), vmem((2 * NT, PAD), BF16), vmem((NI, DESC), F32),
    ]
    deep = (3, 4, 3)
    scratch += [vmem((d, 64, 128), F32) for d in deep]
    scratch += [vmem((N_TRAIN, d, 8, 128), F32) for d in deep]
    scratch += [vmem((d, 64, 128), F32) for d in deep]
    scratch += [vmem((12, 8, 128), F32)] * 2
    scratch += [vmem((N_PLANE, 2, 8, 128), F32)] * 2
    scratch += [vmem((N_ZHI, 2, 8, 128), F32)] * 2
    scratch += [vmem((12, 8, 128), F32)] * 2
    scratch += [dma((3, N_OWN)), dma((3, N_TRAIN)), dma((3, N_TRAIN)), dma((3, N_OWN))]
    scratch += [dma((2, N_PLANE)), dma((2, N_PLANE)), dma((2, N_ZHI)), dma((2, N_ZHI)), dma((2, N_PLANE)), dma((2, N_PLANE)), dma]
    return pl.pallas_call(
        kernel,
        out_shape=(
            jax.ShapeDtypeStruct((NI, 192), F32),
            jax.ShapeDtypeStruct((NI, 192), F32),
            jax.ShapeDtypeStruct((NI, DESC), F32),
        ),
        in_specs=[whole, whole, whole, whole, pl.BlockSpec(memory_space=pltpu.SMEM)],
        out_specs=(whole, whole, pl.BlockSpec(memory_space=pl.ANY)),
        scratch_shapes=scratch,
        compiler_params=pltpu.CompilerParams(
            collective_id=0, has_side_effects=True, vmem_limit_bytes=48 * 1024 * 1024
        ),
        cost_estimate=pl.CostEstimate(flops=2_000_000_000, bytes_accessed=2_000_000, transcendentals=1_000_000),
    )(train_coords, induce_coords, train_forces, atom_pairs, length_scale)


def solution(mesh):
    in_specs = (P("train", None), P("induce", None), P("train", None), P(), P())
    out_specs = (P("induce", None), P("induce", None), P("induce", None))
    return jax.shard_map(
        per_device, mesh=mesh, in_specs=in_specs, out_specs=out_specs, check_vma=False
    )
```

time: 285 us -> 92.5 us (0.32)
  the two profiles are of different devices: /device:TPU:2 before, /device:TPU:1 now
where the time goes in v1:
time: 92.5 us; the launch traced here: 92.3 us
  Pallas kernels  87.2 us (94%)
  local copies, waits for them, and re-layouts  3.82 us (4%)
  between operations  1.34 us (1%)
    pallas_call x1, Pallas kernels, per_device(): pl.pallas_call(kernel, out_shape=(jax.ShapeDtypeStruct((NI, 192), F32), j...  87.2 us
    pallas_call x3, local copies, waits for them, and re-layouts, per_device(): pl.pallas_call(kernel, out_shape=(jax.ShapeDtypeStruct((NI, 192), F32), j...  2.78 us

profile of v1, /device:TPU:1, one launch (start us, length us, event | category | flops | bytes accessed | tf_op | source)
XLA Modules:
  0.0 92.3 jit_solution(10735687019208977067)
XLA Ops:
  1.3 0.0 copy-start
  1.3 0.0 copy-start.1
  1.3 0.0 copy-start.2
  1.3 1.0 %copy.8.ic = f32[128,192]{1,0:T(8,128)S(1)} copy(f32[128,192]{0,1:T(8,128)} %param.6) | data formatting | bytes 196608 | tf_op args[1]
  2.4 0.0 copy-done
  2.4 0.0 copy-done.1
  2.4 0.0 copy-done.2
  2.4 87.2 %shard_map.76 = (f32[128,192]{1,0:T(8,128)S(1)}, f32[128,192]{1,0:T(8,128)S(1)}, f32[128,2016]{1,0:T(8,128)S(1)}) custom-call(f32[64,192]{1,0:T(8,128)S(1)} %copy-done, f32[128,192]{1,0:T(8,128)S(1)} %copy.8.ic, f32[64,192]{1,0:T(8,128)S(1)} %copy-done.1, s32[2,2016]{1,0:T(2,128)S(1)} %copy-done.2, f32[1]{0:T(128)S(6)} %copy.12.scale), custom_call_target="tpu_custom_call" | custom-call | flops 2000000000 | bytes 2000000 | tf_op jit(solution)/shard_map/pallas_call | solution.py:459
  89.6 0.7 copy.9
  90.3 0.7 copy.10
  91.0 1.3 %copy.11 = f32[128,2016]{0,1:T(8,128)} copy(f32[128,2016]{1,0:T(8,128)S(1)} %get-tuple-element.5) | data formatting | bytes 2064384 | tf_op jit(solution)/shard_map/pallas_call | solution.py:459
Async XLA Ops:
  1.3 1.1 %copy-start = (f32[64,192]{1,0:T(8,128)S(1)}, f32[64,192]{1,0:T(8,128)}, u32[]{:S(2)}) copy-start(f32[64,192]{1,0:T(8,128)} %tc.1) | copy-start | bytes 147460
  1.3 1.1 %copy-start.1 = (f32[64,192]{1,0:T(8,128)S(1)}, f32[64,192]{1,0:T(8,128)}, u32[]{:S(2)}) copy-start(f32[64,192]{1,0:T(8,128)} %tf.1) | copy-start | bytes 147460
  1.3 1.1 %copy-start.2 = (s32[2,2016]{1,0:T(2,128)S(1)}, s32[2,2016]{1,0:T(2,128)}, u32[]{:S(2)}) copy-start(s32[2,2016]{1,0:T(2,128)} %pairs.1) | copy-start | bytes 48388

commit v2 on v1

--- a/solution.py
+++ b/solution.py
@@ -13,7 +13,8 @@
 ROOT5 = math.sqrt(5.0)
 ATOMS, DESC, PAD = 64, 2016, 2048
 NT, NI = 64, 128
-TILE = 512
+TILE = 1024
+DESC_PART = 504
 TILES = [pl.ds(j * TILE, TILE) for j in range(PAD // TILE)]
 N_TRAIN, N_OWN = 16, 8
 OWN0 = 4
@@ -36,7 +37,9 @@
 def pack(wide):
     half = wide.shape[0] // 2
     left = wide[:, 0:128]
-    right = jnp.concatenate([wide[:, 128:192], jnp.zeros((wide.shape[0], 64), F32)], axis=1)
+    right = wide[:, 128:256]
+    if right.shape[1] < 128:
+        right = jnp.concatenate([right, jnp.zeros((wide.shape[0], 64), F32)], axis=1)
     left_turned, right_turned = pltpu.roll(left, 64, 1), pltpu.roll(right, 64, 1)
     low = lane_of((half, 128)) < 64
     return [
@@ -47,13 +50,9 @@
 
 
 def unpack_into(ref, planes):
-    half = planes[0].shape[0]
-    low = lane_of((half, 128)) < 64
-    turned = [pltpu.roll(p, 64, 1) for p in planes]
-    ref[0:half, 0:128] = jnp.where(low, planes[0], turned[1])
-    ref[half : 2 * half, 0:128] = jnp.where(low, turned[0], planes[1])
-    ref[0:half, 128:192] = planes[2][:, 0:64]
-    ref[half : 2 * half, 128:192] = turned[2][:, 0:64]
+    for c, plane in enumerate(planes):
+        both = jnp.concatenate([plane, pltpu.roll(plane, 64, 1)], axis=0)
+        ref[c * ATOMS : (c + 1) * ATOMS, :] = both.T[0:ATOMS]
 
 
 def two_parts(full):
@@ -72,13 +71,14 @@
 
 
 def kernel(
-    tc, ic, tf, pairs, scale,
+    tc_far, ic_far, tf_far, pairs_far, scale,
+    far_coeff, far_resid, far_desc,
     out_coeff, out_resid, out_desc,
-    ends, inc, inc_t, grad_t, grad_i, z, vu, vw, desc,
+    tc, ic, tf, pairs, ends, inc, inc_t, grad_t, grad_i, z, vu, vw,
     s_part0, s_part1, s_part2, s_in0, s_in1, s_in2, s_all0, s_all1, s_all2,
     p_part0, p_part1, p_in0, p_in1, p_z0, p_z1, p_all0, p_all1,
     rs_send, rs_recv, ag_send, ag_recv,
-    pr_send, pr_recv, pz_send, pz_recv, pg_send, pg_recv, desc_sem,
+    pr_send, pr_recv, pz_send, pz_recv, pg_send, pg_recv, load_sem, store_sem,
 ):
     s_part, s_in, s_all = [s_part0, s_part1, s_part2], [s_in0, s_in1, s_in2], [s_all0, s_all1, s_all2]
     p_part, p_in, p_z, p_all = [p_part0, p_part1], [p_in0, p_in1], [p_z0, p_z1], [p_all0, p_all1]
@@ -93,6 +93,13 @@
     def in_column(other):
         return (t, x * 8 + other * 2 + core)
 
+    loads = [
+        pltpu.make_async_copy(source, target, load_sem.at[k])
+        for k, (source, target) in enumerate(((pairs_far, pairs), (ic_far, ic), (tc_far, tc), (tf_far, tf)))
+    ]
+    for load in loads:
+        load.start()
+
     barrier = pltpu.get_barrier_semaphore()
     for d in range(1, N_TRAIN):
         pl.semaphore_signal(barrier, inc=1, device_id=(lax.rem(t + d, N_TRAIN), i), device_id_type=MESH)
@@ -100,6 +107,9 @@
         pl.semaphore_signal(barrier, inc=1, device_id=in_plane(lax.rem(spot + d, N_PLANE)), device_id_type=MESH)
     for d in range(1, N_ZHI):
         pl.semaphore_signal(barrier, inc=1, device_id=in_column(lax.rem(zh + d, N_ZHI)), device_id_type=MESH)
+
+    for load in loads:
+        load.wait()
 
     ends[...] = jnp.full((2, PAD), -1, jnp.int32)
     ends[:, 0:DESC] = pairs[...]
@@ -135,7 +145,7 @@
         [jnp.where(first8, jnp.broadcast_to(points, (8, 128)), 0.0) for points in lattice], axis=0
     )
     lattice_rows = jnp.concatenate([lattice_rows, jnp.zeros((24, 128), F32)], axis=1).astype(BF16)
-    rows_t, rows_i = coordinate_rows(pack(tc[...])), coordinate_rows(pack(ic[...]))
+    rows_t, rows_i = coordinate_rows(pack(tc[...])), coordinate_rows(pack(jnp.concatenate([ic[...], jnp.zeros((64, NI), F32)], axis=0).T))
 
     def describe(rows, tile, last):
         n = rows.shape[0] // 3
@@ -228,12 +238,29 @@
             total = total + to_forces(h, grad_i, tile)
         return packed_planes(total)
 
-    is_owner = jnp.logical_and(t >= OWN0, t < OWN0 + N_OWN)
+    z_lo, y = t // 4, lax.rem(t, 4)
+    is_owner = jnp.logical_or(z_lo == 1, z_lo == 2)
     mine = lax.rem(t + N_OWN - OWN0, N_OWN)
+    far = jnp.where(z_lo <= 1, 2, 1)
+    near = 3 - far
+    to_owners = [(far, 2), (near, 2), (far, 1), (far, 3), (near, 1), (near, 3), (far, 0), (near, 0)]
+    end = jnp.where(z_lo == 1, 3, 0)
+    inner, edge = 3 - z_lo, 3 - end
+    to_all = [
+        (end, 2), (end, 1), (end, 3), (inner, 2), (edge, 2), (end, 0), (inner, 1), (inner, 3),
+        (edge, 1), (edge, 3), (z_lo, 2), (inner, 0), (edge, 0), (z_lo, 1), (z_lo, 3),
+    ]
     waits = []
+
+    def spot_of(step):
+        return step[0] * 4 + lax.rem(y + step[1], 4)
 
     def chunk_rows(k):
         return pl.ds(pl.multiple_of(k * 8, 8), 8)
+
+    def drain():
+        while waits:
+            waits.pop(0)()
 
     def sum_over_train(n, planes, extra=None):
         part, arrived, everything = s_part[n], s_in[n], s_all[n]
@@ -244,32 +271,34 @@
                 part[3, k * 8 : (k + 1) * 8, :] = extra
 
         def scatter(d):
-            k = lax.rem(mine + d, N_OWN)
+            owner = spot_of(to_owners[d])
             return pltpu.make_async_remote_copy(
-                src_ref=part.at[:, chunk_rows(k), :], dst_ref=arrived.at[t],
+                src_ref=part.at[:, chunk_rows(owner - OWN0), :], dst_ref=arrived.at[t],
                 send_sem=rs_send.at[n, d], recv_sem=rs_recv.at[n, t],
-                device_id=(k + OWN0, i), device_id_type=MESH,
+                device_id=(owner, i), device_id_type=MESH,
             )
 
         def gather(d):
             return pltpu.make_async_remote_copy(
                 src_ref=everything.at[:, chunk_rows(mine), :], dst_ref=everything.at[:, chunk_rows(mine), :],
                 send_sem=ag_send.at[n, d], recv_sem=ag_recv.at[n, mine],
-                device_id=(lax.rem(t + d, N_TRAIN), i), device_id_type=MESH,
+                device_id=(spot_of(to_all[d]), i), device_id_type=MESH,
             )
 
-        for d in range(1, N_OWN):
+        for d in range(N_OWN - 1):
             scatter(d).start()
 
         @pl.when(jnp.logical_not(is_owner))
         def _():
-            scatter(0).start()
+            scatter(N_OWN - 1).start()
+
+        drain()
 
         @pl.when(is_owner)
         def _():
             total = part[:, chunk_rows(mine), :]
-            for d in range(1, N_TRAIN):
-                source = lax.rem(t + d, N_TRAIN)
+            for step in reversed(to_all):
+                source = spot_of(step)
                 pltpu.make_async_remote_copy(
                     src_ref=part.at[:, chunk_rows(mine), :], dst_ref=arrived.at[source],
                     send_sem=rs_send.at[n, 0], recv_sem=rs_recv.at[n, source],
@@ -277,7 +306,7 @@
                 ).wait_recv()
                 total = total + arrived[source]
             everything[:, chunk_rows(mine), :] = total
-            for d in range(1, N_TRAIN):
+            for d in range(N_TRAIN - 1):
                 gather(d).start()
 
         def arrive():
@@ -293,22 +322,26 @@
             return [everything[c] for c in range(3)]
 
         def finish():
-            for d in range(1, N_OWN):
+            for d in range(N_OWN - 1):
                 scatter(d).wait_send()
 
             @pl.when(jnp.logical_not(is_owner))
             def _():
-                scatter(0).wait_send()
+                scatter(N_OWN - 1).wait_send()
 
             @pl.when(is_owner)
             def _():
-                for d in range(1, N_TRAIN):
+                for d in range(N_TRAIN - 1):
                     gather(d).wait_send()
 
         waits.append(finish)
         return arrive
 
-    has_chunk = spot < P_OWN
+    has_chunk = x < P_OWN // 2
+    in_plane_steps = [(2, 0), (2, 1), (1, 0), (3, 0), (1, 1), (3, 1), (0, 1)]
+
+    def plane_spot(step):
+        return lax.rem(x + step[0], 4) * 2 + lax.rem(core + step[1], 2)
 
     def sum_over_induce(n, planes):
         part, arrived, column, everything = p_part[n], p_in[n], p_z[n], p_all[n]
@@ -320,7 +353,7 @@
             return pl.ds(k * 2, 2)
 
         def scatter(d):
-            k = lax.rem(spot + d, P_OWN)
+            k = plane_spot(in_plane_steps[d])
             return pltpu.make_async_remote_copy(
                 src_ref=part.at[pair_of(k)], dst_ref=arrived.at[spot],
                 send_sem=pr_send.at[n, d], recv_sem=pr_recv.at[n, spot],
@@ -338,21 +371,23 @@
             return pltpu.make_async_remote_copy(
                 src_ref=everything.at[pair_of(spot)], dst_ref=everything.at[pair_of(spot)],
                 send_sem=pg_send.at[n, d], recv_sem=pg_recv.at[n, spot],
-                device_id=in_plane(lax.rem(spot + d, N_PLANE)), device_id_type=MESH,
+                device_id=in_plane(plane_spot(in_plane_steps[d])), device_id_type=MESH,
             )
 
-        for d in range(1, P_OWN):
-            scatter(d).start()
-
-        @pl.when(jnp.logical_not(has_chunk))
-        def _():
-            scatter(0).start()
+        def for_owners(act):
+            for d, step in enumerate(in_plane_steps):
+                @pl.when(plane_spot(step) < P_OWN)
+                def _():
+                    act(d)
+
+        for_owners(lambda d: scatter(d).start())
+        drain()
 
         @pl.when(has_chunk)
         def _():
             total = part[pair_of(spot)]
-            for d in range(1, N_PLANE):
-                source = lax.rem(spot + d, N_PLANE)
+            for step in reversed(in_plane_steps):
+                source = plane_spot(step)
                 pltpu.make_async_remote_copy(
                     src_ref=part.at[pair_of(spot)], dst_ref=arrived.at[source],
                     send_sem=pr_send.at[n, 0], recv_sem=pr_recv.at[n, source],
@@ -362,7 +397,7 @@
             column[zh] = total
             for d in (2, 1, 3):
                 across(d).start()
-            for d in range(1, N_ZHI):
+            for d in (1, 3, 2):
                 source = lax.rem(zh + d, N_ZHI)
                 pltpu.make_async_remote_copy(
                     src_ref=column.at[zh], dst_ref=column.at[source],
@@ -370,33 +405,29 @@
                     device_id=in_column(source), device_id_type=MESH,
                 ).wait_recv()
             everything[pair_of(spot)] = (column[0] + column[1]) + (column[2] + column[3])
-            for d in range(1, N_PLANE):
+            for d in range(N_PLANE - 1):
                 gather(d).start()
 
+        def arrived_from(d):
+            k = plane_spot(in_plane_steps[d])
+            pltpu.make_async_remote_copy(
+                src_ref=everything.at[pair_of(k)], dst_ref=everything.at[pair_of(k)],
+                send_sem=pg_send.at[n, 0], recv_sem=pg_recv.at[n, k],
+                device_id=in_plane(k), device_id_type=MESH,
+            ).wait_recv()
+
         def arrive():
-            for k in range(P_OWN):
-                @pl.when(spot != k)
-                def _():
-                    pltpu.make_async_remote_copy(
-                        src_ref=everything.at[pair_of(k)], dst_ref=everything.at[pair_of(k)],
-                        send_sem=pg_send.at[n, 0], recv_sem=pg_recv.at[n, k],
-                        device_id=in_plane(k), device_id_type=MESH,
-                    ).wait_recv()
+            for_owners(arrived_from)
             return [everything[c * 4 : (c + 1) * 4].reshape(32, 128) for c in range(3)]
 
         def finish():
-            for d in range(1, P_OWN):
-                scatter(d).wait_send()
-
-            @pl.when(jnp.logical_not(has_chunk))
-            def _():
-                scatter(0).wait_send()
+            for_owners(lambda d: scatter(d).wait_send())
 
             @pl.when(has_chunk)
             def _():
                 for d in range(1, N_ZHI):
                     across(d).wait_send()
-                for d in range(1, N_PLANE):
+                for d in range(N_PLANE - 1):
                     gather(d).wait_send()
 
         waits.append(finish)
@@ -428,23 +459,47 @@
     rows = spread(coeffs)
     for j, tile in enumerate(TILES):
         width = min(TILE, DESC - j * TILE)
-        desc[:, pl.ds(j * TILE, width)] = to_desc(rows, grad_i, tile)[:, 0:width]
-    copy = pltpu.make_async_copy(desc, out_desc, desc_sem)
-    copy.start()
+        out_desc[pl.ds(j * TILE, width), :] = to_desc(rows, grad_i, tile).T[0:width]
+    stores = [
+        pltpu.make_async_copy(source, target, store_sem.at[k])
+        for k, (source, target) in enumerate(((out_desc, far_desc), (out_coeff, far_coeff), (out_resid, far_resid)))
+    ]
+    stores[0].start()
+    stores[1].start()
     final = sum_over_train(2, adjoint(arrive()))()
     unpack_into(out_resid, [a - b for a, b in zip(residual, final)])
-    for finish in waits:
-        finish()
-    copy.wait()
+    stores[2].start()
+    drain()
+    for store in stores:
+        store.wait()
+
+
+def write_out(coeffs, resid, desc, out_coeffs, out_resid, out_desc, via_coeffs, via_resid, via_desc, in_sem, out_sem):
+    parts = [(desc, via_desc, out_desc, k * DESC_PART, DESC_PART) for k in range(DESC // DESC_PART)]
+    parts += [(coeffs, via_coeffs, out_coeffs, 0, 192), (resid, via_resid, out_resid, 0, 192)]
+    ins, outs = [], []
+    for k, (source, via, target, at, size) in enumerate(parts):
+        rows = pl.ds(at, size)
+        ins.append(pltpu.make_async_copy(source.at[rows], via.at[rows], in_sem.at[k]))
+        outs.append(pltpu.make_async_copy(via.at[rows], target.at[rows], out_sem.at[k]))
+    for copy in ins:
+        copy.start()
+    for first, second in zip(ins, outs):
+        first.wait()
+        second.start()
+    for copy in outs:
+        copy.wait()
 
 
 def per_device(train_coords, induce_coords, train_forces, atom_pairs, length_scale):
     vmem, dma = pltpu.VMEM, pltpu.SemaphoreType.DMA
     whole = pl.BlockSpec(memory_space=pltpu.VMEM)
-    scratch = [
+    scratch = [vmem((192, NI), F32), vmem((192, NI), F32), vmem((DESC, NI), F32)]
+    scratch += [
+        vmem((NT, 192), F32), vmem((192, NI), F32), vmem((NT, 192), F32), vmem((2, DESC), jnp.int32),
         vmem((2, PAD), jnp.int32), vmem((256, PAD), BF16), vmem((PAD, 128), BF16),
         vmem((3, NT, PAD), F32), vmem((3, NI, PAD), F32),
-        vmem((NT + NI, PAD), BF16), vmem((2 * NI, PAD), BF16), vmem((2 * NT, PAD), BF16), vmem((NI, DESC), F32),
+        vmem((NT + NI, PAD), BF16), vmem((2 * NI, PAD), BF16), vmem((2 * NT, PAD), BF16),
     ]
     deep = (3, 4, 3)
     scratch += [vmem((d, 64, 128), F32) for d in deep]
@@ -455,22 +510,30 @@
     scratch += [vmem((N_ZHI, 2, 8, 128), F32)] * 2
     scratch += [vmem((12, 8, 128), F32)] * 2
     scratch += [dma((3, N_OWN)), dma((3, N_TRAIN)), dma((3, N_TRAIN)), dma((3, N_OWN))]
-    scratch += [dma((2, N_PLANE)), dma((2, N_PLANE)), dma((2, N_ZHI)), dma((2, N_ZHI)), dma((2, N_PLANE)), dma((2, N_PLANE)), dma]
-    return pl.pallas_call(
+    scratch += [dma((2, N_PLANE)), dma((2, N_PLANE)), dma((2, N_ZHI)), dma((2, N_ZHI)), dma((2, N_PLANE)), dma((2, N_PLANE)), dma((4,)), dma((3,))]
+    results = pl.pallas_call(
         kernel,
         out_shape=(
-            jax.ShapeDtypeStruct((NI, 192), F32),
-            jax.ShapeDtypeStruct((NI, 192), F32),
-            jax.ShapeDtypeStruct((NI, DESC), F32),
+            jax.ShapeDtypeStruct((192, NI), F32),
+            jax.ShapeDtypeStruct((192, NI), F32),
+            jax.ShapeDtypeStruct((DESC, NI), F32),
         ),
-        in_specs=[whole, whole, whole, whole, pl.BlockSpec(memory_space=pltpu.SMEM)],
-        out_specs=(whole, whole, pl.BlockSpec(memory_space=pl.ANY)),
+        in_specs=[pl.BlockSpec(memory_space=pltpu.HBM)] * 4 + [pl.BlockSpec(memory_space=pltpu.SMEM)],
+        out_specs=(pl.BlockSpec(memory_space=pltpu.HBM),) * 3,
         scratch_shapes=scratch,
         compiler_params=pltpu.CompilerParams(
-            collective_id=0, has_side_effects=True, vmem_limit_bytes=48 * 1024 * 1024
+            collective_id=0, has_side_effects=True, vmem_limit_bytes=63 * 1024 * 1024
         ),
         cost_estimate=pl.CostEstimate(flops=2_000_000_000, bytes_accessed=2_000_000, transcendentals=1_000_000),
-    )(train_coords, induce_coords, train_forces, atom_pairs, length_scale)
+    )(train_coords, induce_coords.T, train_forces, atom_pairs, length_scale)
+    coeffs, resid, desc = pl.pallas_call(
+        write_out,
+        out_shape=[jax.ShapeDtypeStruct(r.shape, r.dtype) for r in results],
+        in_specs=[pl.BlockSpec(memory_space=pltpu.HBM)] * 3,
+        out_specs=[pl.BlockSpec(memory_space=pltpu.HBM)] * 3,
+        scratch_shapes=[vmem(r.shape, r.dtype) for r in results] + [dma((DESC // DESC_PART + 2,))] * 2,
+    )(*results)
+    return coeffs.T, resid.T, desc.T
 
 
 def solution(mesh):

time: 92.5 us -> 87.2 us (0.943)
  local copies, waits for them, and re-layouts: 3.82 us -> 0 us
  Pallas kernels: 87.2 us -> 85.7 us
    pallas_call x3 -> x0, local copies, waits for them, and re-layouts: 2.78 us -> none  [per_device(): pl.pallas_call(kernel, out_shape=(jax.ShapeDtypeStruct((NI, 192), F32), j...]
    pallas_call x1 -> x2, Pallas kernels: 87.2 us -> 85.7 us  [the longest x1 83.5 us: per_device(): pl.pallas_call(kernel, out_shape=(jax.ShapeDtypeStruct((192, NI), F32), j...]
    unnamed x7 -> x0, local copies, waits for them, and re-layouts: 1.05 us -> none
where the time goes in v2:
time: 87.2 us; the launch traced here: 87 us
  Pallas kernels  85.7 us (98%)
  between operations  1.29 us (1%)
    pallas_call x1, Pallas kernels, per_device(): pl.pallas_call(kernel, out_shape=(jax.ShapeDtypeStruct((192, NI), F32), j...  83.5 us
    pallas_call x1, Pallas kernels, per_device(): pl.pallas_call(write_out, out_shape=[jax.ShapeDtypeStruct(r.shape, r.dtyp...  2.19 us

profile of v2, /device:TPU:1, one launch (start us, length us, event | category | flops | bytes accessed | tf_op | source)
XLA Modules:
  0.0 87.0 jit_solution(8249243980261031260)
XLA Ops:
  1.3 83.5 %shard_map.76 = (f32[192,128]{1,0:T(8,128)}, f32[192,128]{1,0:T(8,128)}, f32[2016,128]{1,0:T(8,128)}) custom-call(f32[64,192]{1,0:T(8,128)} %tc_far.1, f32[192,128]{1,0:T(8,128)} %bitcast.5, f32[64,192]{1,0:T(8,128)} %tf_far.1, s32[2,2016]{1,0:T(2,128)} %pairs_far.1, f32[1]{0:T(128)S(6)} %copy.8.scale), custom_call_target="tpu_custom_call" | custom-call | flops 2000000000 | bytes 2000000 | tf_op jit(solution)/shard_map/pallas_call | solution.py:514
  84.8 2.2 %shard_map.77 = (f32[192,128]{1,0:T(8,128)}, f32[192,128]{1,0:T(8,128)}, f32[2016,128]{1,0:T(8,128)}) custom-call(f32[192,128]{1,0:T(8,128)} %get-tuple-element.9.coeffs, f32[192,128]{1,0:T(8,128)} %get-tuple-element.10.resid, f32[2016,128]{1,0:T(8,128)} %get-tuple-element.11.desc), custom_call_target="tpu_custom_call" | custom-call | tf_op jit(solution)/shard_map/pallas_call | solution.py:529

commit v3 on v2

--- a/solution.py
+++ b/solution.py
@@ -74,7 +74,7 @@
     tc_far, ic_far, tf_far, pairs_far, scale,
     far_coeff, far_resid, far_desc,
     out_coeff, out_resid, out_desc,
-    tc, ic, tf, pairs, ends, inc, inc_t, grad_t, grad_i, z, vu, vw,
+    tc, ic, tf, pairs, ends, inc, inc_t, grad_t, grad_i, z, vu, vw, diag_ref, outer_ref, both_ref, sum_ref,
     s_part0, s_part1, s_part2, s_in0, s_in1, s_in2, s_all0, s_all1, s_all2,
     p_part0, p_part1, p_in0, p_in1, p_z0, p_z1, p_all0, p_all1,
     rs_send, rs_recv, ag_send, ag_recv,
@@ -93,6 +93,9 @@
     def in_column(other):
         return (t, x * 8 + other * 2 + core)
 
+    barrier = pltpu.get_barrier_semaphore()
+    for d in (2, 1, 3):
+        pl.semaphore_signal(barrier, inc=1, device_id=in_column(lax.rem(zh + d, N_ZHI)), device_id_type=MESH)
     loads = [
         pltpu.make_async_copy(source, target, load_sem.at[k])
         for k, (source, target) in enumerate(((pairs_far, pairs), (ic_far, ic), (tc_far, tc), (tf_far, tf)))
@@ -100,13 +103,10 @@
     for load in loads:
         load.start()
 
-    barrier = pltpu.get_barrier_semaphore()
     for d in range(1, N_TRAIN):
         pl.semaphore_signal(barrier, inc=1, device_id=(lax.rem(t + d, N_TRAIN), i), device_id_type=MESH)
     for d in range(1, N_PLANE):
         pl.semaphore_signal(barrier, inc=1, device_id=in_plane(lax.rem(spot + d, N_PLANE)), device_id_type=MESH)
-    for d in range(1, N_ZHI):
-        pl.semaphore_signal(barrier, inc=1, device_id=in_column(lax.rem(zh + d, N_ZHI)), device_id_type=MESH)
 
     for load in loads:
         load.wait()
@@ -166,12 +166,11 @@
             for c in range(3):
                 grad[c, :, tile] = off[c] * cube
             z[at : at + n, tile] = (inverse - rest[0:1]).astype(BF16)
-    vu[NI:, :] = z[NT:, :]
     vw[NT:, :] = z[0:NT, :]
 
     length = scale[0]
     gram_t = dot_nt(z[...], z[0:NT, :])
-    gram_i = dot_nt(z[...], z[NT:, :])
+    gram_i = dot_nt(z[NT:, :], z[NT:, :])
 
     def on_diagonal(square, axis):
         rows, columns = square.shape
@@ -186,9 +185,7 @@
             25.0 / (3.0 * (length * length) * (length * length)) * falloff,
         )
 
-    diag, outer = matern(gram_i[0:NT], on_diagonal(gram_t[0:NT], 1), on_diagonal(gram_i[NT:], 0))
-    diag_back, outer_back = matern(gram_t[NT:], on_diagonal(gram_i[NT:], 1), on_diagonal(gram_t[0:NT], 0))
-    diag = diag.astype(BF16)
+    diag_back, outer_back = matern(gram_t[NT:], on_diagonal(gram_i, 1), on_diagonal(gram_t[0:NT], 0))
     diag_back = jnp.concatenate([diag_back, jnp.zeros((NI, 64), F32)], axis=1)
     outer_back = pltpu.roll(jnp.concatenate([outer_back, jnp.zeros((NI, 64), F32)], axis=1), 64, 1)
 
@@ -213,9 +210,9 @@
         for tile in TILES:
             vu[0:NI, tile] = to_desc(rows, grad_i, tile).astype(BF16)
         gram = dot_nt(z[...], vu[0:NI, :])
-        product = outer * (gram[0:NT] - on_diagonal(gram[NT:], 0))
+        product = outer_ref[...] * (gram[0:NT] - on_diagonal(gram[NT:], 0))
         row_sum = jnp.sum(product, axis=1, keepdims=True)
-        both = jnp.concatenate([diag, product.astype(BF16)], axis=1)
+        both = jnp.concatenate([diag_ref[...], product.astype(BF16)], axis=1)
         total = jnp.zeros((3 * NT, 128), F32)
         for tile in TILES:
             w = dot(both, vu[:, tile]) - z[0:NT, tile].astype(F32) * row_sum
@@ -232,10 +229,23 @@
         product = outer_back * (self_dot - gram[NT:])
         col_sum = jnp.sum(product, axis=1, keepdims=True)
         both = jnp.where(lane_of((NI, 128)) < 64, diag_back, -product).astype(BF16)
-        total = jnp.zeros((3 * NI, 128), F32)
+        both_ref[...] = both
+        sum_ref[...] = jnp.broadcast_to(col_sum, (NI, 128))
+
+    def adjoint_half(plane):
+        at = pl.multiple_of(plane * 32, 32)
+        low, high = pl.ds(at, 32), pl.ds(at + 64, 32)
+        both = jnp.concatenate([both_ref[low, :], both_ref[high, :]], axis=0)
+        col_sum = jnp.concatenate([sum_ref[low, :], sum_ref[high, :]], axis=0)[:, 0:1]
+        total = jnp.zeros((3 * 64, 128), F32)
         for tile in TILES:
-            h = dot(both, vw[:, tile]) + z[NT:, tile].astype(F32) * col_sum
-            total = total + to_forces(h, grad_i, tile)
+            own = jnp.concatenate([z[pl.ds(at + NT, 32), tile], z[pl.ds(at + NT + 64, 32), tile]], axis=0)
+            h = dot(both, vw[:, tile]) + own.astype(F32) * col_sum
+            weighted = []
+            for c in range(3):
+                weighted.append((grad_i[c, low, tile] * h[0:32]).astype(BF16))
+                weighted.append((grad_i[c, high, tile] * h[32:64]).astype(BF16))
+            total = total + dot(jnp.concatenate(weighted, axis=0), inc_t[tile, :])
         return packed_planes(total)
 
     z_lo, y = t // 4, lax.rem(t, 4)
@@ -243,7 +253,7 @@
     mine = lax.rem(t + N_OWN - OWN0, N_OWN)
     far = jnp.where(z_lo <= 1, 2, 1)
     near = 3 - far
-    to_owners = [(far, 2), (near, 2), (far, 1), (far, 3), (near, 1), (near, 3), (far, 0), (near, 0)]
+    to_owners = [(far, 2), (far, 1), (far, 3), (far, 0), (near, 2), (near, 1), (near, 3), (near, 0)]
     end = jnp.where(z_lo == 1, 3, 0)
     inner, edge = 3 - z_lo, 3 - end
     to_all = [
@@ -255,37 +265,43 @@
     def spot_of(step):
         return step[0] * 4 + lax.rem(y + step[1], 4)
 
-    def chunk_rows(k):
-        return pl.ds(pl.multiple_of(k * 8, 8), 8)
-
     def drain():
         while waits:
             waits.pop(0)()
 
-    def sum_over_train(n, planes, extra=None):
+    def adjoint_over_train(n, vector, extra=None, before=lambda: None, meanwhile=False):
         part, arrived, everything = s_part[n], s_in[n], s_all[n]
-        for c in range(3):
-            part[c] = planes[c]
-        if extra is not None:
-            for k in range(N_OWN):
-                part[3, k * 8 : (k + 1) * 8, :] = extra
+        adjoint(vector)
+
+        def fill(plane):
+            planes = adjoint_half(plane)
+            for k in range(4):
+                for c in range(3):
+                    part[plane * 4 + k, c] = planes[c][k * 8 : (k + 1) * 8]
+                if extra is not None:
+                    part[plane * 4 + k, 3] = extra
 
         def scatter(d):
             owner = spot_of(to_owners[d])
             return pltpu.make_async_remote_copy(
-                src_ref=part.at[:, chunk_rows(owner - OWN0), :], dst_ref=arrived.at[t],
+                src_ref=part.at[owner - OWN0], dst_ref=arrived.at[t],
                 send_sem=rs_send.at[n, d], recv_sem=rs_recv.at[n, t],
                 device_id=(owner, i), device_id_type=MESH,
             )
 
         def gather(d):
             return pltpu.make_async_remote_copy(
-                src_ref=everything.at[:, chunk_rows(mine), :], dst_ref=everything.at[:, chunk_rows(mine), :],
+                src_ref=everything.at[mine], dst_ref=everything.at[mine],
                 send_sem=ag_send.at[n, d], recv_sem=ag_recv.at[n, mine],
                 device_id=(spot_of(to_all[d]), i), device_id_type=MESH,
             )
 
-        for d in range(N_OWN - 1):
+        fill(far - 1)
+        before()
+        for d in range(4):
+            scatter(d).start()
+        fill(near - 1)
+        for d in range(4, N_OWN - 1):
             scatter(d).start()
 
         @pl.when(jnp.logical_not(is_owner))
@@ -293,19 +309,26 @@
             scatter(N_OWN - 1).start()
 
         drain()
+        if meanwhile:
+            vu[NI:, :] = z[NT:, :]
+            diag, outer = matern(
+                dot_nt(z[0:NT, :], z[NT:, :]), on_diagonal(gram_t[0:NT], 1), on_diagonal(gram_i, 0)
+            )
+            diag_ref[...] = diag.astype(BF16)
+            outer_ref[...] = outer
 
         @pl.when(is_owner)
         def _():
-            total = part[:, chunk_rows(mine), :]
+            total = part[mine]
             for step in reversed(to_all):
                 source = spot_of(step)
                 pltpu.make_async_remote_copy(
-                    src_ref=part.at[:, chunk_rows(mine), :], dst_ref=arrived.at[source],
+                    src_ref=part.at[mine], dst_ref=arrived.at[source],
                     send_sem=rs_send.at[n, 0], recv_sem=rs_recv.at[n, source],
                     device_id=(source, i), device_id_type=MESH,
                 ).wait_recv()
                 total = total + arrived[source]
-            everything[:, chunk_rows(mine), :] = total
+            everything[mine] = total
             for d in range(N_TRAIN - 1):
                 gather(d).start()
 
@@ -313,13 +336,12 @@
             for k in range(N_OWN):
                 @pl.when(t != k + OWN0)
                 def _():
-                    rows = pl.ds(k * 8, 8)
                     pltpu.make_async_remote_copy(
-                        src_ref=everything.at[:, rows, :], dst_ref=everything.at[:, rows, :],
+                        src_ref=everything.at[k], dst_ref=everything.at[k],
                         send_sem=ag_send.at[n, 0], recv_sem=ag_recv.at[n, k],
                         device_id=(k + OWN0, i), device_id_type=MESH,
                     ).wait_recv()
-            return [everything[c] for c in range(3)]
+            return [everything[:, c].reshape(64, 128) for c in range(3)]
 
         def finish():
             for d in range(N_OWN - 1):
@@ -438,14 +460,16 @@
         return jnp.sum(line, axis=1, keepdims=True)
 
     forces = pack(tf[...])
-    first = adjoint(forces)
-    pl.semaphore_wait(barrier, N_TRAIN - 1 + N_PLANE - 1 + N_ZHI - 1)
-    start = sum_over_train(0, first)()
+
+    def everyone_is_in():
+        pl.semaphore_wait(barrier, N_TRAIN - 1 + N_PLANE - 1 + N_ZHI - 1)
+
+    start = adjoint_over_train(0, forces, before=everyone_is_in, meanwhile=True)()
     probed = sum_over_induce(0, forward(start))()
     row8 = lax.broadcasted_iota(jnp.int32, (8, 128), 0)
     sums = jnp.where(row8 == 0, whole_sum(probed, probed), whole_sum(forces, probed))
-    again = sum_over_train(1, adjoint(probed), sums)()
-    quotient = s_all1[3, 0:1, 0:1] / s_all1[3, 1:2, 0:1]
+    again = adjoint_over_train(1, probed, sums)()
+    quotient = s_all1[0, 3, 0:1, 0:1] / s_all1[0, 3, 1:2, 0:1]
     center = 0.775 * quotient
     spread_ = 0.725 * quotient
     momentum = spread_ / center
@@ -466,7 +490,7 @@
     ]
     stores[0].start()
     stores[1].start()
-    final = sum_over_train(2, adjoint(arrive()))()
+    final = adjoint_over_train(2, arrive())()
     unpack_into(out_resid, [a - b for a, b in zip(residual, final)])
     stores[2].start()
     drain()
@@ -500,11 +524,13 @@
         vmem((2, PAD), jnp.int32), vmem((256, PAD), BF16), vmem((PAD, 128), BF16),
         vmem((3, NT, PAD), F32), vmem((3, NI, PAD), F32),
         vmem((NT + NI, PAD), BF16), vmem((2 * NI, PAD), BF16), vmem((2 * NT, PAD), BF16),
+        vmem((NT, NI), BF16), vmem((NT, NI), F32),
+        vmem((NI, NI), BF16), vmem((NI, 128), F32),
     ]
     deep = (3, 4, 3)
-    scratch += [vmem((d, 64, 128), F32) for d in deep]
+    scratch += [vmem((N_OWN, d, 8, 128), F32) for d in deep]
     scratch += [vmem((N_TRAIN, d, 8, 128), F32) for d in deep]
-    scratch += [vmem((d, 64, 128), F32) for d in deep]
+    scratch += [vmem((N_OWN, d, 8, 128), F32) for d in deep]
     scratch += [vmem((12, 8, 128), F32)] * 2
     scratch += [vmem((N_PLANE, 2, 8, 128), F32)] * 2
     scratch += [vmem((N_ZHI, 2, 8, 128), F32)] * 2

time: 87.2 us -> 87.3 us (level)
  no operation moved by 1% of the time
where the time goes in v3:
time: 87.3 us; the launch traced here: 87.1 us
  Pallas kernels  85.9 us (98%)
  between operations  1.29 us (1%)
    pallas_call x1, Pallas kernels, per_device(): pl.pallas_call(kernel, out_shape=(jax.ShapeDtypeStruct((192, NI), F32), j...  83.7 us
    pallas_call x1, Pallas kernels, per_device(): pl.pallas_call(write_out, out_shape=[jax.ShapeDtypeStruct(r.shape, r.dtyp...  2.19 us

profile of v3, /device:TPU:1, one launch (start us, length us, event | category | flops | bytes accessed | tf_op | source)
XLA Modules:
  0.0 87.1 jit_solution(15655499826401014208)
XLA Ops:
  1.3 83.7 %shard_map.76 = (f32[192,128]{1,0:T(8,128)}, f32[192,128]{1,0:T(8,128)}, f32[2016,128]{1,0:T(8,128)}) custom-call(f32[64,192]{1,0:T(8,128)} %tc_far.1, f32[192,128]{1,0:T(8,128)} %bitcast.5, f32[64,192]{1,0:T(8,128)} %tf_far.1, s32[2,2016]{1,0:T(2,128)} %pairs_far.1, f32[1]{0:T(128)S(6)} %copy.8.scale), custom_call_target="tpu_custom_call" | custom-call | flops 2000000000 | bytes 2000000 | tf_op jit(solution)/shard_map/pallas_call | solution.py:540
  84.9 2.2 %shard_map.77 = (f32[192,128]{1,0:T(8,128)}, f32[192,128]{1,0:T(8,128)}, f32[2016,128]{1,0:T(8,128)}) custom-call(f32[192,128]{1,0:T(8,128)} %get-tuple-element.9.coeffs, f32[192,128]{1,0:T(8,128)} %get-tuple-element.10.resid, f32[2016,128]{1,0:T(8,128)} %get-tuple-element.11.desc), custom_call_target="tpu_custom_call" | custom-call | tf_op jit(solution)/shard_map/pallas_call | solution.py:555
